TPU v7x, 512 devices: a whole 4x8x8 slice. The times are simulated.
512 devices in a mesh: section: 32 (over z, x_hi, core), tensor: 16 (over x_lo, y).
Axes of the slice: x: 4 (x_hi: 2, x_lo: 2; x = x_hi * 2 + x_lo), y: 8, z: 8, core: 2. Of those that a mesh axis runs over, the one named last changes fastest.
Arguments:
- fwd_qkv: bfloat16 [32, 3, 480, 6144], P('section', None, None, 'tensor'), may hold values from -4 to 4
- stash: bfloat16 [32, 1, 3, 480, 6144], P('section', None, None, None, 'tensor'), may hold values from -4 to 4
- out_grad: bfloat16 [32, 480, 6144], P('section', None, 'tensor'), may hold values from -6 to 6
- norm_gain: float32 [6144], P('tensor'), may hold values from 0.1 to 1.9
- read_slot: int32 [32], replicated, may hold values from 0 to 1
- write_slot: int32 [32], replicated, may hold values from 0 to 1, as said below
Outputs:
- handed_act: bfloat16 [32, 480, 6144], P('section', None, 'tensor')
- handed_grad: bfloat16 [32, 3, 480, 6144], P('section', None, None, 'tensor')
- new_stash: bfloat16 [32, 1, 3, 480, 6144], P('section', None, None, None, 'tensor')
Inputs may be any that keep to these rules, and one draw needn't show every extreme that they name: `write_slot`: the two sections of a pair, p and 31 - p, always name different slots.
All inputs are finite; a program needn't handle non-finite values.
Results may differ from a plain program's by a relative error of at most 0.015.
Values may be sent and summed in bfloat16 or wider, within the bound.
A program may use at most 64 MiB of HBM per device.

v0:
```python
import jax
import jax.numpy as jnp
from jax import lax
from jax.sharding import PartitionSpec as P

HD = 128


NORM_EPS = 1e-05


def shifted(value, axis, steps):
    count = lax.axis_size(axis)
    first, last = (max(0, -steps), min(count, count - steps))
    return lax.ppermute(value, axis, [(source, source + steps) for source in range(first, last)])


def attend(query, keys_in, values_in):
    length = query.shape[0]
    q_heads = query.reshape(length, -1, HD)
    k_heads = keys_in.reshape(length, -1, HD)
    v_heads = values_in.reshape(length, -1, HD)
    scores = jnp.einsum(
        "qhd,khd->hqk", q_heads, k_heads, preferred_element_type=jnp.float32
    ) * HD ** (-0.5)
    positions = jnp.arange(length, dtype=jnp.int32)
    causal = positions[:, None] >= positions[None, :]
    scores = jnp.where(causal[None], scores, jnp.float32(-1e30))
    top_score = jnp.max(scores, axis=-1, keepdims=True)
    exp_terms = jnp.exp(scores - top_score)
    soft_probs = exp_terms / jnp.sum(exp_terms, axis=-1, keepdims=True)
    probs_low = soft_probs.astype(jnp.bfloat16)
    attended = jnp.einsum(
        "hqk,khd->qhd", probs_low, v_heads, preferred_element_type=jnp.float32
    ).reshape(length, -1)
    return (soft_probs, probs_low, attended)


def attend_back(query, keys_in, values_in, soft_probs, probs_low, attended, grad_att):
    length = query.shape[0]
    q_heads = query.reshape(length, -1, HD)
    k_heads = keys_in.reshape(length, -1, HD)
    v_heads = values_in.reshape(length, -1, HD)
    g_heads = grad_att.reshape(length, -1, HD)
    a_heads = attended.reshape(length, -1, HD)
    grad_probs = jnp.einsum("qhd,khd->hqk", g_heads, v_heads, preferred_element_type=jnp.float32)
    grad_values = jnp.einsum("hqk,qhd->khd", probs_low, g_heads, preferred_element_type=jnp.float32)
    row_delta = jnp.transpose(jnp.sum(g_heads.astype(jnp.float32) * a_heads, axis=-1))
    grad_scores = (soft_probs * (grad_probs - row_delta[:, :, None]) * HD ** (-0.5)).astype(
        jnp.bfloat16
    )
    grad_query = jnp.einsum(
        "hqk,khd->qhd", grad_scores, k_heads, preferred_element_type=jnp.float32
    )
    grad_keys = jnp.einsum("hqk,qhd->khd", grad_scores, q_heads, preferred_element_type=jnp.float32)
    return (
        grad_query.astype(jnp.bfloat16).reshape(length, -1),
        grad_keys.astype(jnp.bfloat16).reshape(length, -1),
        grad_values.astype(jnp.bfloat16).reshape(length, -1),
    )


def shards(fwd_qkv, stash, out_grad, norm_gain, read_slot, write_slot):
    section_count = lax.axis_size("section")
    section_here = lax.axis_index("section")
    partner = section_count - 1 - section_here
    lower_half = section_here < section_count // 2
    slot_count = stash.shape[1]

    def held_here(slot_id):
        return (slot_id < slot_count) == lower_half

    own_read = read_slot[section_here]
    their_read = read_slot[partner]
    own_write = write_slot[section_here]
    their_write = write_slot[partner]
    local_slots = stash[0]
    forward_in = fwd_qkv[0]
    requested = lax.dynamic_index_in_dim(local_slots, their_read % slot_count, 0, keepdims=False)
    row_count = forward_in.shape[1]
    col_count = forward_in.shape[2]
    pieces = (3, section_count, row_count // section_count, col_count)
    spread_fwd, spread_slot = (
        lax.all_to_all(
            forward_in.reshape(pieces), "section", split_axis=1, concat_axis=1, tiled=True
        ),
        lax.all_to_all(
            requested.reshape(pieces), "section", split_axis=1, concat_axis=1, tiled=True
        ),
    )
    back_fwd, back_slot = (
        lax.all_to_all(jnp.flip(spread_fwd, 1), "section", split_axis=1, concat_axis=1, tiled=True),
        lax.all_to_all(
            jnp.flip(spread_slot, 1), "section", split_axis=1, concat_axis=1, tiled=True
        ),
    )
    got_fwd = back_fwd.reshape(forward_in.shape)
    got_slot = back_slot.reshape(forward_in.shape)
    own_copy = lax.dynamic_index_in_dim(local_slots, own_read % slot_count, 0, keepdims=False)
    backward_in = jnp.where(held_here(own_read), own_copy, got_slot)
    slot_ids = jnp.arange(slot_count, dtype=jnp.int32)[:, None, None, None]
    renewed = jnp.where(
        (slot_ids == own_write % slot_count) & held_here(own_write), forward_in[None], local_slots
    )
    renewed = jnp.where(
        (slot_ids == their_write % slot_count) & held_here(their_write), got_fwd[None], renewed
    )
    unused_a, unused_b, out_fwd = attend(forward_in[0], forward_in[1], forward_in[2])
    soft_probs, probs_low, out_back = attend(backward_in[0], backward_in[1], backward_in[2])
    width_all = norm_gain.shape[0] * lax.axis_size("tensor")
    sq_fwd, sq_back = lax.psum(
        (jnp.sum(out_fwd * out_fwd, axis=-1), jnp.sum(out_back * out_back, axis=-1)), "tensor"
    )
    inv_fwd = lax.rsqrt(sq_fwd / width_all + NORM_EPS)
    inv_back = lax.rsqrt(sq_back / width_all + NORM_EPS)
    handed = (out_fwd * inv_fwd[:, None] * norm_gain).astype(jnp.bfloat16)
    scaled_grad = out_grad[0].astype(jnp.float32) * norm_gain
    row_dot = lax.psum(jnp.sum(scaled_grad * out_back, axis=-1), "tensor") / width_all
    grad_att = (
        inv_back[:, None] * scaled_grad - out_back * (inv_back**3 * row_dot)[:, None]
    ).astype(jnp.bfloat16)
    grad_query, grad_keys, grad_values = attend_back(
        backward_in[0], backward_in[1], backward_in[2], soft_probs, probs_low, out_back, grad_att
    )
    moved_act = shifted(handed, "section", 1)
    moved_query, moved_keys, moved_values = shifted(
        (grad_query, grad_keys, grad_values), "section", -1
    )
    return (
        moved_act[None],
        jnp.stack([moved_query, moved_keys, moved_values])[None],
        renewed[None],
    )


def solution(mesh):
    in_specs = (
        P("section", None, None, "tensor"),
        P("section", None, None, None, "tensor"),
        P("section", None, "tensor"),
        P("tensor"),
        P(),
        P(),
    )
    out_specs = (
        P("section", None, "tensor"),
        P("section", None, None, "tensor"),
        P("section", None, None, None, "tensor"),
    )
    return jax.shard_map(shards, mesh=mesh, in_specs=in_specs, out_specs=out_specs, check_vma=False)
```

profile of v0, /device:TPU:64, one launch (start us, length us, event | category | flops | bytes accessed | tf_op | source)
XLA Modules:
  0.0 222.1 jit_solution(15427396766570677965)
XLA Ops:
  3.2 12.7 %all-to-all-start = ((bf16[3,32,15,384]{3,2,0,1:T(8,128)(2,1)}), bf16[3,32,15,384]{3,2,0,1:T(8,128)(2,1)S(1)}, u32[]{:S(2)}, u32[]{:S(2)}) async-start(bf16[3,32,15,384]{3,2,0,1:T(8,128)(2,1)} %copy.48), calls=%async_computation | async-start | bytes 2359296 | tf_op jit(solution)/shard_map/all_to_all | solution.py:87
  17.2 2.4 %copy.67 = bf16[3,32,15,384]{3,2,0,1:T(8,128)(2,1)} copy(bf16[3,32,15,384]{3,2,1,0:T(8,128)(2,1)} %reshape_squeeze.30) | data formatting | bytes 2211840 | tf_op jit(solution)/shard_map/reshape;squeeze | solution.py:85
  19.6 27.2 %all-to-all-done = bf16[3,32,15,384]{3,2,0,1:T(8,128)(2,1)S(1)} async-done(((bf16[3,32,15,384]{3,2,0,1:T(8,128)(2,1)}), bf16[3,32,15,384]{3,2,0,1:T(8,128)(2,1)S(1)}, u32[]{:S(2)}, u32[]{:S(2)}) %all-to-all-start) | async-done | bytes 1105952 | tf_op jit(solution)/shard_map/all_to_all | solution.py:87
  47.8 5.9 %all-to-all-start.2 = ((bf16[3,32,15,384]{3,2,0,1:T(8,128)(2,1)}), bf16[3,32,15,384]{3,2,0,1:T(8,128)(2,1)S(1)}, u32[]{:S(2)}, u32[]{:S(2)}) async-start(bf16[3,32,15,384]{3,2,0,1:T(8,128)(2,1)} %copy.67), calls=%async_computation.2 | async-start | bytes 2359296 | tf_op jit(solution)/shard_map/all_to_all | solution.py:84
  53.7 2.4 %rev.7 = bf16[3,32,15,384]{3,2,0,1:T(8,128)(2,1)} reverse(bf16[3,32,15,384]{3,2,0,1:T(8,128)(2,1)} %copy-done.5), dimensions={1} | reverse | bytes 2211840 | tf_op jit(solution)/shard_map/jit(_flip)/rev | solution.py:94
  56.1 28.4 %all-to-all-done.2 = bf16[3,32,15,384]{3,2,0,1:T(8,128)(2,1)S(1)} async-done(((bf16[3,32,15,384]{3,2,0,1:T(8,128)(2,1)}), bf16[3,32,15,384]{3,2,0,1:T(8,128)(2,1)S(1)}, u32[]{:S(2)}, u32[]{:S(2)}) %all-to-all-start.2) | async-done | bytes 1105952 | tf_op jit(solution)/shard_map/all_to_all | solution.py:84
  84.6 5.9 %all-to-all-start.1 = ((bf16[3,32,15,384]{3,2,0,1:T(8,128)(2,1)}), bf16[3,32,15,384]{3,2,0,1:T(8,128)(2,1)}, u32[]{:S(2)}, u32[]{:S(2)}) async-start(bf16[3,32,15,384]{3,2,0,1:T(8,128)(2,1)} %rev.7), calls=%async_computation.1 | async-start | bytes 2359296 | tf_op jit(solution)/shard_map/all_to_all | solution.py:93
  93.0 2.9 %fusion.32 = (f32[3,480]{1,0:T(4,128)S(1)}, f32[3,480,480]{1,2,0:T(8,128)}) fusion(pred[480,480]{0,1:T(8,128)(4,1)S(1)} %iota_compare_fusion, bf16[480,3,128]{0,2,1:T(8,128)(2,1)S(1)} %bitcast.83, bf16[480,3,128]{0,2,1:T(8,128)(2,1)S(1)} %bitcast.84), kind=kOutput, calls=%fused_computation.54 | convolution fusion | flops 179712480 | bytes 3738240 | tf_op jit(solution)/shard_map/sub | solution.py:30
  95.9 2.6 %multiply_reduce_fusion.3 = (f32[480]{0:T(512)S(1)}, f32[480,3,128]{2,0,1:T(8,128)S(1)}) fusion(bf16[480,3,128]{0,2,1:T(8,128)(2,1)S(1)} %bitcast.82, f32[3,480,480]{1,2,0:T(8,128)} %get-tuple-element.27, f32[3,480]{1,0:T(4,128)S(1)} %get-tuple-element.26), kind=kOutput, calls=%fused_computation.40 | convolution fusion | flops 178697760 | bytes 3878400 | tf_op jit(solution)/shard_map/hqk,khd->qhd/dot_general | solution.py:33
  101.6 2.5 %rev.8 = bf16[3,32,15,384]{3,2,0,1:T(8,128)(2,1)} reverse(bf16[3,32,15,384]{3,2,0,1:T(8,128)(2,1)} %copy-done.4), dimensions={1} | reverse | bytes 2211840 | tf_op jit(solution)/shard_map/jit(_flip)/rev | solution.py:92
  104.1 17.4 %all-to-all-done.1 = bf16[3,32,15,384]{3,2,0,1:T(8,128)(2,1)} async-done(((bf16[3,32,15,384]{3,2,0,1:T(8,128)(2,1)}), bf16[3,32,15,384]{3,2,0,1:T(8,128)(2,1)}, u32[]{:S(2)}, u32[]{:S(2)}) %all-to-all-start.1) | async-done | bytes 1105952 | tf_op jit(solution)/shard_map/all_to_all | solution.py:93
  121.4 5.9 %all-to-all-start.3 = ((bf16[3,32,15,384]{3,2,0,1:T(8,128)(2,1)}), bf16[3,32,15,384]{3,2,0,1:T(8,128)(2,1)}, u32[]{:S(2)}, u32[]{:S(2)}) async-start(bf16[3,32,15,384]{3,2,0,1:T(8,128)(2,1)} %rev.8), calls=%async_computation.3 | async-start | bytes 2359296 | tf_op jit(solution)/shard_map/all_to_all | solution.py:92
  127.3 2.4 %copy.49 = bf16[3,32,15,384]{3,2,1,0:T(8,128)(2,1)} copy(bf16[3,32,15,384]{3,2,0,1:T(8,128)(2,1)} %all-to-all-done.1) | data formatting | bytes 2211840 | tf_op jit(solution)/shard_map/all_to_all | solution.py:93
  129.8 2.3 %reshape.92 = bf16[3,480,384]{2,1,0:T(8,128)(2,1)} reshape(bf16[3,32,15,384]{3,2,1,0:T(8,128)(2,1)} %copy.49) | data formatting | bytes 2211840 | tf_op jit(solution)/shard_map/reshape | solution.py:98
  138.5 4.0 %fusion.33 = (f32[3,480]{1,0:T(4,128)S(1)}, f32[3,480,480]{1,2,0:T(8,128)}) fusion(pred[480,480]{0,1:T(8,128)(4,1)} %copy-done.12, bf16[480,3,128]{0,2,1:T(8,128)(2,1)S(1)} %bitcast.71, bf16[480,3,128]{0,2,1:T(8,128)(2,1)} %bitcast.73), kind=kOutput, calls=%fused_computation.55 | convolution fusion | flops 179712480 | bytes 3738240 | tf_op jit(solution)/shard_map/sub | solution.py:30
  142.5 2.3 %fusion.12 = bf16[3,480,480]{1,2,0:T(8,128)(2,1)S(1)} fusion(f32[3,480,480]{1,2,0:T(8,128)} %get-tuple-element.31, f32[3,480]{1,0:T(4,128)S(1)} %get-tuple-element.30), kind=kLoop, calls=%fused_computation.23 | loop fusion | flops 1382400 | bytes 4152960 | tf_op jit(solution)/shard_map/convert_element_type | solution.py:32
  146.4 34.6 %all-reduce = (f32[480]{0:T(512)S(1)}, f32[480]{0:T(512)S(1)}, f32[480]{0:T(512)S(1)}) all-reduce(f32[480]{0:T(512)S(1)} %get-tuple-element.28, f32[480]{0:T(512)S(1)} %get-tuple-element.10, f32[480]{0:T(512)S(1)} %get-tuple-element.9), channel_id=1, replica_groups=mesh['section'=32,'tensor'=16] {'tensor'}, use_global_device_ids=true, to_apply=%region_3.4 | all-reduce | flops 1440 | bytes 11520 | tf_op jit(solution)/shard_map/psum | solution.py:111
  181.1 2.2 fusion.19
  189.6 6.2 %collective-permute-start.3 = (bf16[480,384]{0,1:T(8,128)(2,1)}, bf16[480,384]{0,1:T(8,128)(2,1)}, u32[]{:S(2)}, u32[]{:S(2)}) collective-permute-start(bf16[480,384]{0,1:T(8,128)(2,1)} %bitcast.79), channel_id=1, source_target_pairs={{16,0},{32,16},{48,32},{64,48},{80,64},{96,80},{112,96},{128,112},... | collective-permute-start | bytes 1105928 | tf_op jit(solution)/shard_map/ppermute | solution.py:15
  195.8 2.6 %multiply_convert_fusion = bf16[3,480,480]{1,2,0:T(8,128)(2,1)S(1)} fusion(bf16[480,3,128]{2,0,1:T(8,128)(2,1)} %copy-done.11, bf16[480,3,128]{0,2,1:T(8,128)(2,1)S(1)} %bitcast.76, f32[3,480]{1,0:T(4,128)S(1)} %bitcast.87, f32[3,480,480]{1,2,0:T(8,128)} %get-tuple-element.31, f32[3,480]{1,0:T(4,128)S(1)} %get-tuple-element.30), kind=kOutput, calls=%fused_computation.2 | convolution fusion | flops 180403200 | bytes 4896000 | tf_op jit(solution)/shard_map/qhd,khd->hqk/dot_general | solution.py:46
  205.2 4.6 %collective-permute-start.1 = (bf16[480,384]{0,1:T(8,128)(2,1)}, bf16[480,384]{0,1:T(8,128)(2,1)S(1)}, u32[]{:S(2)}, u32[]{:S(2)}) collective-permute-start(bf16[480,384]{0,1:T(8,128)(2,1)} %bitcast.81), channel_id=1, source_target_pairs={{16,0},{32,16},{48,32},{64,48},{80,64},{96,80},{112,96},{128,112},... | collective-permute-start | bytes 1105928 | tf_op jit(solution)/shard_map/ppermute | solution.py:15
  211.7 2.4 %copy.68 = bf16[3,32,15,384]{3,2,1,0:T(8,128)(2,1)} copy(bf16[3,32,15,384]{3,2,0,1:T(8,128)(2,1)} %all-to-all-done.3) | data formatting | bytes 2211840 | tf_op jit(solution)/shard_map/all_to_all | solution.py:92
  214.2 2.2 %broadcast_in_dim_reshape.3 = bf16[1,3,480,384]{3,2,1,0:T(8,128)(2,1)} reshape(bf16[3,32,15,384]{3,2,1,0:T(8,128)(2,1)} %copy.68) | data formatting | bytes 2211840 | tf_op jit(solution)/shard_map/broadcast_in_dim;reshape | solution.py:106
  217.6 1.9 copy.69
  (70 shorter events, 35.1 us)
Async XLA Ops:
  3.2 12.7 %copy-start = (bf16[1,3,480,384]{3,2,1,0:T(8,128)(2,1)S(1)}, bf16[1,3,480,384]{3,2,1,0:T(8,128)(2,1)}, u32[]{:S(2)}) copy-start(bf16[1,3,480,384]{3,2,1,0:T(8,128)(2,1)} %param.6) | copy-start | bytes 3317764
  3.2 43.6 %all-to-all-start = ((bf16[3,32,15,384]{3,2,0,1:T(8,128)(2,1)}), bf16[3,32,15,384]{3,2,0,1:T(8,128)(2,1)S(1)}, u32[]{:S(2)}, u32[]{:S(2)}) async-start(bf16[3,32,15,384]{3,2,0,1:T(8,128)(2,1)} %copy.48), calls=%async_computation | async-start | bytes 2359296 | tf_op jit(solution)/shard_map/all_to_all | solution.py:87
  46.8 1.0 copy-start.5
  47.8 36.7 %all-to-all-start.2 = ((bf16[3,32,15,384]{3,2,0,1:T(8,128)(2,1)}), bf16[3,32,15,384]{3,2,0,1:T(8,128)(2,1)S(1)}, u32[]{:S(2)}, u32[]{:S(2)}) async-start(bf16[3,32,15,384]{3,2,0,1:T(8,128)(2,1)} %copy.67), calls=%async_computation.2 | async-start | bytes 2359296 | tf_op jit(solution)/shard_map/all_to_all | solution.py:84
  84.6 6.8 %copy-start.4 = (bf16[3,32,15,384]{3,2,0,1:T(8,128)(2,1)}, bf16[3,32,15,384]{3,2,0,1:T(8,128)(2,1)S(1)}, u32[]{:S(2)}) copy-start(bf16[3,32,15,384]{3,2,0,1:T(8,128)(2,1)S(1)} %all-to-all-done.2) | copy-start | bytes 3317764
  84.6 36.8 %all-to-all-start.1 = ((bf16[3,32,15,384]{3,2,0,1:T(8,128)(2,1)}), bf16[3,32,15,384]{3,2,0,1:T(8,128)(2,1)}, u32[]{:S(2)}, u32[]{:S(2)}) async-start(bf16[3,32,15,384]{3,2,0,1:T(8,128)(2,1)} %rev.7), calls=%async_computation.1 | async-start | bytes 2359296 | tf_op jit(solution)/shard_map/all_to_all | solution.py:93
  93.0 2.9 %copy-start.12 = (pred[480,480]{0,1:T(8,128)(4,1)}, pred[480,480]{0,1:T(8,128)(4,1)S(1)}, u32[]{:S(2)}) copy-start(pred[480,480]{0,1:T(8,128)(4,1)S(1)} %iota_compare_fusion) | copy-start | bytes 691204
  98.5 1.2 copy-start.10
  99.7 0.7 copy-start.15
  121.4 90.3 %all-to-all-start.3 = ((bf16[3,32,15,384]{3,2,0,1:T(8,128)(2,1)}), bf16[3,32,15,384]{3,2,0,1:T(8,128)(2,1)}, u32[]{:S(2)}, u32[]{:S(2)}) async-start(bf16[3,32,15,384]{3,2,0,1:T(8,128)(2,1)} %rev.8), calls=%async_computation.3 | async-start | bytes 2359296 | tf_op jit(solution)/shard_map/all_to_all | solution.py:92
  129.8 2.3 %copy-start.1 = (bf16[1,1,3,480,384]{4,3,2,1,0:T(8,128)(2,1)S(1)}, bf16[1,1,3,480,384]{4,3,2,1,0:T(8,128)(2,1)}, u32[]{:S(2)}) copy-start(bf16[1,1,3,480,384]{4,3,2,1,0:T(8,128)(2,1)} %param.7) | copy-start | bytes 3317764
  142.5 2.3 %copy-start.8 = (bf16[1,480,384]{1,2,0:T(8,128)(2,1)S(1)}, bf16[1,480,384]{1,2,0:T(8,128)(2,1)}, u32[]{:S(2)}) copy-start(bf16[1,480,384]{1,2,0:T(8,128)(2,1)} %copy.54) | copy-start | bytes 1105924
  142.5 2.3 %copy-start.13 = (f32[384]{0:T(512)S(1)}, f32[384]{0:T(512)}, u32[]{:S(2)}) copy-start(f32[384]{0:T(512)} %param.9) | copy-start | bytes 4612
  144.8 1.6 copy-start.2
  181.1 4.1 %copy-start.6 = (f32[480,3,128]{2,0,1:T(8,128)S(1)}, f32[480,3,128]{2,0,1:T(8,128)}, u32[]{:S(2)}) copy-start(f32[480,3,128]{2,0,1:T(8,128)} %get-tuple-element.32) | copy-start | bytes 2211844
  181.1 5.3 %copy-start.3 = (bf16[3,480,480]{1,2,0:T(8,128)(2,1)S(1)}, bf16[3,480,480]{1,2,0:T(8,128)(2,1)}, u32[]{:S(2)}) copy-start(bf16[3,480,480]{1,2,0:T(8,128)(2,1)} %copy-done.2) | copy-start | bytes 4147204
  183.3 34.4 %collective-permute-start = (bf16[480,384]{0,1:T(8,128)(2,1)}, bf16[480,384]{0,1:T(8,128)(2,1)}, u32[]{:S(2)}, u32[]{:S(2)}) collective-permute-start(bf16[480,384]{0,1:T(8,128)(2,1)} %fusion.19), channel_id=1, source_target_pairs={{0,16},{16,32},{32,48},{48,64},{64,80},{80,96},{96,112},{112,128},... | collective-permute-start | bytes 1105928 | tf_op jit(solution)/shard_map/ppermute | solution.py:15
  185.7 0.7 copy-start.11
  186.4 9.4 %copy-start.9 = (bf16[1,480,384]{1,2,0:T(8,128)(2,1)S(1)}, bf16[1,480,384]{1,2,0:T(8,128)(2,1)}, u32[]{:S(2)}) copy-start(bf16[1,480,384]{1,2,0:T(8,128)(2,1)} %copy.54) | copy-start | bytes 1105924
  189.6 30.0 %collective-permute-start.3 = (bf16[480,384]{0,1:T(8,128)(2,1)}, bf16[480,384]{0,1:T(8,128)(2,1)}, u32[]{:S(2)}, u32[]{:S(2)}) collective-permute-start(bf16[480,384]{0,1:T(8,128)(2,1)} %bitcast.79), channel_id=1, source_target_pairs={{16,0},{32,16},{48,32},{64,48},{80,64},{96,80},{112,96},{128,112},... | collective-permute-start | bytes 1105928 | tf_op jit(solution)/shard_map/ppermute | solution.py:15
  198.5 1.3 copy-start.7
  199.8 10.1 %copy-start.14 = (s32[32]{0:T(128)S(1)}, s32[32]{0:T(128)}, u32[]{:S(2)}) copy-start(s32[32]{0:T(128)} %param.11) | copy-start | bytes 388
  202.4 17.2 %collective-permute-start.2 = (bf16[480,384]{0,1:T(8,128)(2,1)}, bf16[480,384]{0,1:T(8,128)(2,1)S(1)}, u32[]{:S(2)}, u32[]{:S(2)}) collective-permute-start(bf16[480,384]{0,1:T(8,128)(2,1)} %bitcast.80), channel_id=1, source_target_pairs={{16,0},{32,16},{48,32},{64,48},{80,64},{96,80},{112,96},{128,112},... | collective-permute-start | bytes 1105928 | tf_op jit(solution)/shard_map/ppermute | solution.py:15
  205.2 14.4 %collective-permute-start.1 = (bf16[480,384]{0,1:T(8,128)(2,1)}, bf16[480,384]{0,1:T(8,128)(2,1)S(1)}, u32[]{:S(2)}, u32[]{:S(2)}) collective-permute-start(bf16[480,384]{0,1:T(8,128)(2,1)} %bitcast.81), channel_id=1, source_target_pairs={{16,0},{32,16},{48,32},{64,48},{80,64},{96,80},{112,96},{128,112},... | collective-permute-start | bytes 1105928 | tf_op jit(solution)/shard_map/ppermute | solution.py:15
where the time goes:
time: 224 us; the launch traced here: 222 us
  waiting for transfers between devices  73 us (33%)
  starting transfers between devices  45.1 us (20%)
  local copies, waits for them, and re-layouts  40.7 us (18%)
  blocking collectives  34.6 us (15%)
  matrix products  17 us (8%)
  other arithmetic  8.81 us (4%)
  between operations  2.91 us (1%)
    psum x1, blocking collectives, shards(): lax.psum((jnp.sum(out_fwd * out_fwd, axis=-1), jnp.sum(out_back * out_bac...  34.6 us
    all_to_all x1, waiting for transfers between devices, shards(): lax.all_to_all(forward_in.reshape(pieces), 'section', split_axis=1, conca...  28.4 us
    all_to_all x1, waiting for transfers between devices, shards(): lax.all_to_all(requested.reshape(pieces), 'section', split_axis=1, concat...  27.2 us
    all_to_all x1, waiting for transfers between devices, shards(): lax.all_to_all(jnp.flip(spread_slot, 1), 'section', split_axis=1, concat_...  17.4 us
    ppermute x4, starting transfers between devices, shifted(): lax.ppermute(value, axis, [(source, source + steps) for source in range(f...  14.7 us
    all_to_all x1, starting transfers between devices, shards(): lax.all_to_all(requested.reshape(pieces), 'section', split_axis=1, concat...  12.7 us
    sub x2, matrix products, attend(): exp_terms = jnp.exp(scores - top_score)  6.88 us
    all_to_all x1, starting transfers between devices, shards(): lax.all_to_all(jnp.flip(spread_fwd, 1), 'section', split_axis=1, concat_a...  5.92 us
  transfers between devices with their start and end apart: 8, of which 3 were waited for; matrix products, arithmetic and copies ran while one was open for 27% of the time, Pallas kernels for 0%

commit v1 on v0

v1 whole, which is shorter than its diff:
```python
import functools

import jax
import jax.numpy as jnp
from jax import lax
from jax.experimental import pallas as pl
from jax.experimental.pallas import tpu as pltpu
from jax.sharding import PartitionSpec as P

HD = 128
NORM_EPS = 1e-05
SCALE = HD ** (-0.5)
MESH = pl.DeviceIdType.MESH
F32 = jnp.float32
BF16 = jnp.bfloat16


def cols(head):
    return pl.ds(head * HD, HD)


def nt(a, b):
    return lax.dot_general(a, b, (((1,), (1,)), ((), ())), preferred_element_type=F32)


def nn(a, b):
    return lax.dot_general(a, b, (((1,), (0,)), ((), ())), preferred_element_type=F32)


def tn(a, b):
    return lax.dot_general(a, b, (((0,), (0,)), ((), ())), preferred_element_type=F32)


def attend(q, k, v):
    length = q.shape[0]
    scores = nt(q, k) * SCALE
    rows = lax.broadcasted_iota(jnp.int32, (length, length), 0)
    keys = lax.broadcasted_iota(jnp.int32, (length, length), 1)
    scores = jnp.where(rows >= keys, scores, F32(-1e30))
    terms = jnp.exp(scores - jnp.max(scores, axis=-1, keepdims=True))
    probs = terms * (1.0 / jnp.sum(terms, axis=-1, keepdims=True))
    low = probs.astype(BF16)
    return probs, low, nn(low, v)


def kernel(
    n_sec, n_ten, width_all,
    flags_ref, fwd_ref, stash_ref, og_ref, gain_ref,
    act_ref, grad_ref, new_ref,
    got_s, got_f, act_out, grad_out, att_f, att_b, probs_ref, low_ref, part, wide, tiles_f, tiles_b,
    s_send, s_recv, f_send, f_recv, g_send, g_recv, a_send, a_recv, pf_send, pf_recv, pb_send, pb_recv,
):
    length = og_ref.shape[0]
    heads = og_ref.shape[1] // HD
    me_s = lax.axis_index("section")
    me_t = lax.axis_index("tensor")
    partner = (n_sec - 1 - me_s, me_t)
    up = (me_s + 1, me_t)
    down = (me_s - 1, me_t)
    has_up = me_s < n_sec - 1
    has_down = me_s > 0

    barrier = pltpu.get_barrier_semaphore()

    def greet(device):
        pl.semaphore_signal(barrier, inc=1, device_id=device, device_id_type=MESH)

    greet(partner)
    greet((lax.rem(me_s + 1, n_sec), me_t))
    greet((lax.rem(me_s + n_sec - 1, n_sec), me_t))

    def greet_peer(step, carry):
        greet((me_s, lax.rem(me_t + step, n_ten)))
        return carry

    lax.fori_loop(1, n_ten, greet_peer, 0)
    pl.semaphore_wait(barrier, n_ten + 2)

    def copy_to(src, dst, send, recv, device):
        return pltpu.make_async_remote_copy(
            src_ref=src, dst_ref=dst, send_sem=send, recv_sem=recv, device_id=device, device_id_type=MESH
        )

    def stash_copy(h):
        return copy_to(
            stash_ref.at[:, :, cols(h)], got_s.at[:, :, cols(h)], s_send.at[h], s_recv.at[h], partner
        )

    def fwd_copy(h):
        return copy_to(
            fwd_ref.at[:, :, cols(h)], got_f.at[:, :, cols(h)], f_send.at[h], f_recv.at[h], partner
        )

    def grad_copy(h):
        return copy_to(
            grad_out.at[:, :, cols(h)], grad_ref.at[:, :, cols(h)], g_send.at[h], g_recv.at[h], down
        )

    def act_copy():
        return copy_to(act_out, act_ref, a_send.at[0], a_recv.at[0], up)

    def spread(tiles, send, recv):
        def start(step, carry):
            peer = lax.rem(me_t + step, n_ten)
            copy_to(tiles.at[me_t], tiles.at[me_t], send.at[step], recv.at[me_t], (me_s, peer)).start()
            return carry

        lax.fori_loop(1, n_ten, start, 0)

    def collect(tiles, send, recv):
        def finish(step, carry):
            peer = lax.rem(me_t + step, n_ten)
            copy_to(tiles.at[me_t], tiles.at[me_t], send.at[step], recv.at[me_t], (me_s, peer)).wait_send()
            copy_to(tiles.at[peer], tiles.at[peer], send.at[step], recv.at[peer], (me_s, peer)).wait_recv()
            return carry

        lax.fori_loop(1, n_ten, finish, 0)
        return jnp.sum(tiles[...], axis=0)

    def token_sums(tile, row, partial):
        wide[0:length, :] = partial
        for block in range(4):
            summed = jnp.sum(jnp.transpose(wide[block * HD : (block + 1) * HD, :]), axis=0, keepdims=True)
            tile[row + block : row + block + 1, :] = summed

    def per_token(rows):
        blocks = [
            jnp.transpose(jnp.broadcast_to(rows[b : b + 1, :], (HD, HD))) for b in range(4)
        ]
        return jnp.concatenate(blocks, axis=0)[0:length, :]

    for h in range(heads):
        stash_copy(h).start()

    wide[...] = jnp.zeros_like(wide)
    tiles_f[me_t] = jnp.zeros((8, HD), F32)

    squares = jnp.zeros((length, HD), F32)
    for h in range(heads):
        unused_a, unused_b, out = attend(fwd_ref[0, :, cols(h)], fwd_ref[1, :, cols(h)], fwd_ref[2, :, cols(h)])
        att_f[:, cols(h)] = out
        squares += out * out
    token_sums(part, 0, squares)
    tiles_f[me_t, 0:4, :] = part[0:4, :]
    spread(tiles_f, pf_send, pf_recv)
    total = collect(tiles_f, pf_send, pf_recv)
    inv_fwd = per_token(lax.rsqrt(total[0:4, :] / width_all + NORM_EPS))
    for h in range(heads):
        act_out[:, cols(h)] = (att_f[:, cols(h)] * inv_fwd * gain_ref[0:1, cols(h)]).astype(BF16)
    pl.when(has_up)(lambda: act_copy().start())

    @pl.when(jnp.logical_not(has_down))
    def _():
        act_ref[...] = jnp.zeros_like(act_ref)

    @pl.when(jnp.logical_not(has_up))
    def _():
        grad_ref[...] = jnp.zeros_like(grad_ref)

    own_read = flags_ref[0] > 0
    own_write = flags_ref[1] > 0
    squares = jnp.zeros((length, HD), F32)
    products = jnp.zeros((length, HD), F32)
    for h in range(heads):
        stash_copy(h).wait()
        if h == heads - 1:
            for other in range(heads):
                fwd_copy(other).start()
        for part_at in range(3):
            got_s[part_at, :, cols(h)] = jnp.where(
                own_read, stash_ref[part_at, :, cols(h)], got_s[part_at, :, cols(h)]
            )
        probs, low, out = attend(got_s[0, :, cols(h)], got_s[1, :, cols(h)], got_s[2, :, cols(h)])
        probs_ref[h] = probs
        low_ref[h] = low
        att_b[:, cols(h)] = out
        squares += out * out
        products += og_ref[:, cols(h)].astype(F32) * gain_ref[0:1, cols(h)] * out
    token_sums(part, 0, squares)
    token_sums(part, 4, products)
    tiles_b[me_t] = part[...]
    spread(tiles_b, pb_send, pb_recv)
    total = collect(tiles_b, pb_send, pb_recv)
    inv = lax.rsqrt(total[0:4, :] / width_all + NORM_EPS)
    inv_back = per_token(inv)
    pull = per_token(inv * inv * inv * (total[4:8, :] / width_all))
    for h in range(heads):
        out = att_b[:, cols(h)]
        scaled = og_ref[:, cols(h)].astype(F32) * gain_ref[0:1, cols(h)]
        g_low = (inv_back * scaled - out * pull).astype(BF16)
        grad_probs = nt(g_low, got_s[2, :, cols(h)])
        delta = jnp.sum(g_low.astype(F32) * out, axis=-1, keepdims=True)
        grad_scores = (probs_ref[h] * (grad_probs - delta) * SCALE).astype(BF16)
        grad_out[0, :, cols(h)] = nn(grad_scores, got_s[1, :, cols(h)]).astype(BF16)
        grad_out[1, :, cols(h)] = tn(grad_scores, got_s[0, :, cols(h)]).astype(BF16)
        grad_out[2, :, cols(h)] = tn(low_ref[h], g_low).astype(BF16)
        pl.when(has_down)(lambda: grad_copy(h).start())

    for h in range(heads):
        fwd_copy(h).wait()
        for part_at in range(3):
            new_ref[part_at, :, cols(h)] = jnp.where(
                own_write, fwd_ref[part_at, :, cols(h)], got_f[part_at, :, cols(h)]
            )

    @pl.when(has_up)
    def _():
        act_copy().wait_send()
        for h in range(heads):
            grad_copy(h).wait_recv()

    @pl.when(has_down)
    def _():
        act_copy().wait_recv()
        for h in range(heads):
            grad_copy(h).wait_send()


def shards(fwd_qkv, stash, out_grad, norm_gain, read_slot, write_slot):
    n_sec = lax.axis_size("section")
    n_ten = lax.axis_size("tensor")
    here = lax.axis_index("section")
    slot_count = stash.shape[1]
    lower = here < n_sec // 2
    own_read = (read_slot[here] < slot_count) == lower
    own_write = (write_slot[here] < slot_count) == lower
    flags = jnp.stack([own_read, own_write]).astype(jnp.int32)
    three, length, width = fwd_qkv.shape[1:]
    heads = width // HD
    dma = pltpu.SemaphoreType.DMA
    vmem = pl.BlockSpec(memory_space=pltpu.VMEM)
    act, grads, new = pl.pallas_call(
        functools.partial(kernel, n_sec, n_ten, float(width * n_ten)),
        out_shape=(
            jax.ShapeDtypeStruct((length, width), BF16),
            jax.ShapeDtypeStruct((three, length, width), BF16),
            jax.ShapeDtypeStruct((three, length, width), BF16),
        ),
        in_specs=[pl.BlockSpec(memory_space=pltpu.SMEM)] + [vmem] * 4,
        out_specs=(vmem, vmem, vmem),
        scratch_shapes=[
            pltpu.VMEM((three, length, width), BF16),
            pltpu.VMEM((three, length, width), BF16),
            pltpu.VMEM((length, width), BF16),
            pltpu.VMEM((three, length, width), BF16),
            pltpu.VMEM((length, width), F32),
            pltpu.VMEM((length, width), F32),
            pltpu.VMEM((heads, length, length), F32),
            pltpu.VMEM((heads, length, length), BF16),
            pltpu.VMEM((8, HD), F32),
            pltpu.VMEM((4 * HD, HD), F32),
            pltpu.VMEM((n_ten, 8, HD), F32),
            pltpu.VMEM((n_ten, 8, HD), F32),
            dma((heads,)), dma((heads,)), dma((heads,)), dma((heads,)), dma((heads,)), dma((heads,)),
            dma((1,)), dma((1,)),
            dma((n_ten,)), dma((n_ten,)), dma((n_ten,)), dma((n_ten,)),
        ],
        compiler_params=pltpu.CompilerParams(
            collective_id=0, has_side_effects=True, vmem_limit_bytes=48 * 1024 * 1024
        ),
        name="slot",
    )(flags, fwd_qkv[0], stash[0, 0], out_grad[0], norm_gain[None])
    return act[None], grads[None], new[None, None]


def solution(mesh):
    in_specs = (
        P("section", None, None, "tensor"),
        P("section", None, None, None, "tensor"),
        P("section", None, "tensor"),
        P("tensor"),
        P(),
        P(),
    )
    out_specs = (
        P("section", None, "tensor"),
        P("section", None, None, "tensor"),
        P("section", None, None, None, "tensor"),
    )
    return jax.shard_map(shards, mesh=mesh, in_specs=in_specs, out_specs=out_specs, check_vma=False)
```

time: 224 us -> 142 us (0.63)
  the two profiles are of different devices: /device:TPU:64 before, /device:TPU:449 now
where the time goes in v1:
time: 142 us
  Pallas kernels  130 us (92%)
  local copies, waits for them, and re-layouts  9.36 us (7%)
  between operations  1.97 us (1%)
    pallas_call x1, Pallas kernels, shards(): pl.pallas_call(functools.partial(kernel, n_sec, n_ten, float(width * n_te...  130 us
    unnamed x9, local copies, waits for them, and re-layouts  6.19 us

profile of v1, /device:TPU:449, one launch (start us, length us, event | category | flops | bytes accessed | tf_op | source)
XLA Modules:
  0.0 141.7 jit_solution(12775123837272285717)
XLA Ops:
  0.6 1.2 dynamic_slice.7
  2.5 1.2 dynamic_slice.6
  4.4 0.1 add_convert_fusion.flags_ref
  4.5 0.7 broadcast_in_dim.12.gain_ref
  5.2 0.0 copy-start
  5.2 1.2 copy-done
  6.4 0.0 copy-start.1
  6.5 1.2 copy-done.1
  7.7 0.0 copy-start.2
  7.7 1.0 copy-done.2
  8.7 130.3 %slot.1 = (bf16[480,384]{1,0:T(8,128)(2,1)S(1)}, bf16[3,480,384]{2,1,0:T(8,128)(2,1)S(1)}, bf16[3,480,384]{2,1,0:T(8,128)(2,1)S(1)}) custom-call(s32[2]{0:T(128)S(1)} %add_convert_fusion.flags_ref, bf16[3,480,384]{2,1,0:T(8,128)(2,1)S(1)} %bitcast.10, bf16[3,480,384]{2,1,0:T(8,128)(2,1)S(1)} %bitcast.11, bf16[480,384]{1,0:T(8,128)(2,1)S(1)} %bitcast.14, ...), custom_call_target="tpu_custom_call" | custom-call | tf_op jit(solution)/shard_map/slot/pallas_call | solution.py:232
  139.0 0.7 copy.12
  139.7 1.0 copy.13
  140.7 1.0 copy.14
Async XLA Ops:
  5.2 1.2 copy-start
  6.4 1.2 copy-start.1
  7.7 1.0 copy-start.2

commit v2 on v1

--- a/solution.py
+++ b/solution.py
@@ -10,6 +10,7 @@
 HD = 128
 NORM_EPS = 1e-05
 SCALE = HD ** (-0.5)
+PER_Z = 4
 MESH = pl.DeviceIdType.MESH
 F32 = jnp.float32
 BF16 = jnp.bfloat16
@@ -45,10 +46,10 @@
 
 def kernel(
     n_sec, n_ten, width_all,
-    flags_ref, fwd_ref, stash_ref, og_ref, gain_ref,
-    act_ref, grad_ref, new_ref,
-    got_s, got_f, act_out, grad_out, att_f, att_b, probs_ref, low_ref, part, wide, tiles_f, tiles_b,
-    s_send, s_recv, f_send, f_recv, g_send, g_recv, a_send, a_recv, pf_send, pf_recv, pb_send, pb_recv,
+    read_in, write_in, fwd_in, stash_in, og_in, gain_in,
+    act_ref, grad_ref, new_out,
+    new_ref, zeros, read_ref, write_ref, gain_ref, fwd_ref, stash_ref, og_ref, got_s, got_f, act_out, grad_out, att_f, att_b, probs_ref, low_ref, part, wide, tiles_f, tiles_b,
+    s_send, s_recv, f_send, f_recv, g_send, g_recv, a_send, a_recv, pf_send, pf_recv, pb_send, pb_recv, loads, go_sem,
 ):
     length = og_ref.shape[0]
     heads = og_ref.shape[1] // HD
@@ -59,6 +60,22 @@
     down = (me_s - 1, me_t)
     has_up = me_s < n_sec - 1
     has_down = me_s > 0
+    layer = me_s // PER_Z
+    next_to_middle = lax.rem(layer + 1, 4) < 2
+    z_mate = (me_s + PER_Z * (1 - 2 * lax.rem(layer, 2)), me_t)
+
+    load_stash = pltpu.make_async_copy(stash_in, stash_ref, loads.at[0])
+    load_fwd = pltpu.make_async_copy(fwd_in, fwd_ref, loads.at[1])
+    load_og = pltpu.make_async_copy(og_in, og_ref, loads.at[2])
+    small = [
+        pltpu.make_async_copy(src, dst, loads.at[3 + i])
+        for i, (src, dst) in enumerate(((read_in, read_ref), (write_in, write_ref), (gain_in, gain_ref)))
+    ]
+    load_stash.start()
+    load_fwd.start()
+    load_og.start()
+    for load in small:
+        load.start()
 
     barrier = pltpu.get_barrier_semaphore()
 
@@ -66,6 +83,7 @@
         pl.semaphore_signal(barrier, inc=1, device_id=device, device_id_type=MESH)
 
     greet(partner)
+    greet(z_mate)
     greet((lax.rem(me_s + 1, n_sec), me_t))
     greet((lax.rem(me_s + n_sec - 1, n_sec), me_t))
 
@@ -74,7 +92,8 @@
         return carry
 
     lax.fori_loop(1, n_ten, greet_peer, 0)
-    pl.semaphore_wait(barrier, n_ten + 2)
+    load_stash.wait()
+    pl.semaphore_wait(barrier, n_ten + 3)
 
     def copy_to(src, dst, send, recv, device):
         return pltpu.make_async_remote_copy(
@@ -135,6 +154,10 @@
     wide[...] = jnp.zeros_like(wide)
     tiles_f[me_t] = jnp.zeros((8, HD), F32)
 
+    load_fwd.wait()
+    load_og.wait()
+    for load in small:
+        load.wait()
     squares = jnp.zeros((length, HD), F32)
     for h in range(heads):
         unused_a, unused_b, out = attend(fwd_ref[0, :, cols(h)], fwd_ref[1, :, cols(h)], fwd_ref[2, :, cols(h)])
@@ -146,26 +169,38 @@
     total = collect(tiles_f, pf_send, pf_recv)
     inv_fwd = per_token(lax.rsqrt(total[0:4, :] / width_all + NORM_EPS))
     for h in range(heads):
-        act_out[:, cols(h)] = (att_f[:, cols(h)] * inv_fwd * gain_ref[0:1, cols(h)]).astype(BF16)
+        act_out[:, cols(h)] = (att_f[:, cols(h)] * inv_fwd * gain_ref[cols(h)][None, :]).astype(BF16)
     pl.when(has_up)(lambda: act_copy().start())
 
     @pl.when(jnp.logical_not(has_down))
     def _():
-        act_ref[...] = jnp.zeros_like(act_ref)
+        zeros[...] = jnp.zeros_like(zeros)
+        blank = pltpu.make_async_copy(zeros.at[0], act_ref, loads.at[6])
+        blank.start()
+        blank.wait()
 
     @pl.when(jnp.logical_not(has_up))
     def _():
-        grad_ref[...] = jnp.zeros_like(grad_ref)
-
-    own_read = flags_ref[0] > 0
-    own_write = flags_ref[1] > 0
+        zeros[...] = jnp.zeros_like(zeros)
+        blank = pltpu.make_async_copy(zeros, grad_ref, loads.at[6])
+        blank.start()
+        blank.wait()
+
+    lower = me_s < n_sec // 2
+    own_read = (read_ref[me_s] < 1) == lower
+    own_write = (write_ref[me_s] < 1) == lower
     squares = jnp.zeros((length, HD), F32)
     products = jnp.zeros((length, HD), F32)
     for h in range(heads):
-        stash_copy(h).wait()
         if h == heads - 1:
             for other in range(heads):
-                fwd_copy(other).start()
+                stash_copy(other).wait_send()
+
+            @pl.when(next_to_middle)
+            def _():
+                pl.semaphore_signal(go_sem, inc=1, device_id=z_mate, device_id_type=MESH)
+
+        stash_copy(h).wait_recv()
         for part_at in range(3):
             got_s[part_at, :, cols(h)] = jnp.where(
                 own_read, stash_ref[part_at, :, cols(h)], got_s[part_at, :, cols(h)]
@@ -175,7 +210,7 @@
         low_ref[h] = low
         att_b[:, cols(h)] = out
         squares += out * out
-        products += og_ref[:, cols(h)].astype(F32) * gain_ref[0:1, cols(h)] * out
+        products += og_ref[:, cols(h)].astype(F32) * gain_ref[cols(h)][None, :] * out
     token_sums(part, 0, squares)
     token_sums(part, 4, products)
     tiles_b[me_t] = part[...]
@@ -186,7 +221,7 @@
     pull = per_token(inv * inv * inv * (total[4:8, :] / width_all))
     for h in range(heads):
         out = att_b[:, cols(h)]
-        scaled = og_ref[:, cols(h)].astype(F32) * gain_ref[0:1, cols(h)]
+        scaled = og_ref[:, cols(h)].astype(F32) * gain_ref[cols(h)][None, :]
         g_low = (inv_back * scaled - out * pull).astype(BF16)
         grad_probs = nt(g_low, got_s[2, :, cols(h)])
         delta = jnp.sum(g_low.astype(F32) * out, axis=-1, keepdims=True)
@@ -196,6 +231,12 @@
         grad_out[2, :, cols(h)] = tn(low_ref[h], g_low).astype(BF16)
         pl.when(has_down)(lambda: grad_copy(h).start())
 
+    @pl.when(jnp.logical_not(next_to_middle))
+    def _():
+        pl.semaphore_wait(go_sem, 1)
+
+    for h in range(heads):
+        fwd_copy(h).start()
     for h in range(heads):
         fwd_copy(h).wait()
         for part_at in range(3):
@@ -203,6 +244,9 @@
                 own_write, fwd_ref[part_at, :, cols(h)], got_f[part_at, :, cols(h)]
             )
 
+    store = pltpu.make_async_copy(new_ref, new_out, loads.at[7])
+    store.start()
+
     @pl.when(has_up)
     def _():
         act_copy().wait_send()
@@ -215,16 +259,12 @@
         for h in range(heads):
             grad_copy(h).wait_send()
 
+    store.wait()
+
 
 def shards(fwd_qkv, stash, out_grad, norm_gain, read_slot, write_slot):
     n_sec = lax.axis_size("section")
     n_ten = lax.axis_size("tensor")
-    here = lax.axis_index("section")
-    slot_count = stash.shape[1]
-    lower = here < n_sec // 2
-    own_read = (read_slot[here] < slot_count) == lower
-    own_write = (write_slot[here] < slot_count) == lower
-    flags = jnp.stack([own_read, own_write]).astype(jnp.int32)
     three, length, width = fwd_qkv.shape[1:]
     heads = width // HD
     dma = pltpu.SemaphoreType.DMA
@@ -236,9 +276,17 @@
             jax.ShapeDtypeStruct((three, length, width), BF16),
             jax.ShapeDtypeStruct((three, length, width), BF16),
         ),
-        in_specs=[pl.BlockSpec(memory_space=pltpu.SMEM)] + [vmem] * 4,
-        out_specs=(vmem, vmem, vmem),
+        in_specs=[pl.BlockSpec(memory_space=pl.ANY)] * 6,
+        out_specs=(pl.BlockSpec(memory_space=pl.ANY),) * 3,
         scratch_shapes=[
+            pltpu.VMEM((three, length, width), BF16),
+            pltpu.VMEM((three, length, width), BF16),
+            pltpu.SMEM(read_slot.shape, jnp.int32),
+            pltpu.SMEM(write_slot.shape, jnp.int32),
+            pltpu.VMEM(norm_gain.shape, F32),
+            pltpu.VMEM((three, length, width), BF16),
+            pltpu.VMEM((three, length, width), BF16),
+            pltpu.VMEM((length, width), BF16),
             pltpu.VMEM((three, length, width), BF16),
             pltpu.VMEM((three, length, width), BF16),
             pltpu.VMEM((length, width), BF16),
@@ -254,12 +302,13 @@
             dma((heads,)), dma((heads,)), dma((heads,)), dma((heads,)), dma((heads,)), dma((heads,)),
             dma((1,)), dma((1,)),
             dma((n_ten,)), dma((n_ten,)), dma((n_ten,)), dma((n_ten,)),
+            dma((8,)), pltpu.SemaphoreType.REGULAR,
         ],
         compiler_params=pltpu.CompilerParams(
-            collective_id=0, has_side_effects=True, vmem_limit_bytes=48 * 1024 * 1024
+            collective_id=0, has_side_effects=True, vmem_limit_bytes=56 * 1024 * 1024
         ),
         name="slot",
-    )(flags, fwd_qkv[0], stash[0, 0], out_grad[0], norm_gain[None])
+    )(read_slot, write_slot, fwd_qkv[0], stash[0, 0], out_grad[0], norm_gain)
     return act[None], grads[None], new[None, None]
 
 

time: 142 us -> 133 us (0.937)
  the two profiles are of different devices: /device:TPU:449 before, /device:TPU:199 now
where the time goes in v2:
time: 133 us
  Pallas kernels  127 us (95%)
  local copies, waits for them, and re-layouts  5.19 us (4%)
    pallas_call x1, Pallas kernels, shards(): pl.pallas_call(functools.partial(kernel, n_sec, n_ten, float(width * n_te...  127 us
    unnamed x5, local copies, waits for them, and re-layouts  5.19 us

profile of v2, /device:TPU:199, one launch (start us, length us, event | category | flops | bytes accessed | tf_op | source)
XLA Modules:
  0.0 132.8 jit_solution(9189798450915433175)
XLA Ops:
  0.6 127.0 %slot.1 = (bf16[480,384]{1,0:T(8,128)(2,1)}, bf16[3,480,384]{2,1,0:T(8,128)(2,1)}, bf16[3,480,384]{2,1,0:T(8,128)(2,1)}) custom-call(s32[32]{0:T(128)} %read_in.1, s32[32]{0:T(128)} %write_in.1, bf16[3,480,384]{2,1,0:T(8,128)(2,1)} %bitcast.6, bf16[3,480,384]{2,1,0:T(8,128)(2,1)} %bitcast.7, bf16[480,384]{1,0:T(8,128)(2,1)} %bitcast.10, f32[384]{0:T(512)} %gain_in.1), custom_call_target="tpu_custom_call" | custom-call | tf_op jit(solution)/shard_map/slot/pallas_call | solution.py:272
  127.6 1.8 %copy.12 = bf16[1,480,384]{2,1,0:T(8,128)(2,1)} copy(bf16[1,480,384]{2,1,0:T(8,128)(2,1)} %bitcast.11) | data formatting | bytes 737280
  129.4 0.0 copy-start
  129.4 2.4 %copy.13 = bf16[1,3,480,384]{3,2,1,0:T(8,128)(2,1)} copy(bf16[1,3,480,384]{3,2,1,0:T(8,128)(2,1)} %bitcast.9) | data formatting | bytes 2211840
  131.8 0.0 copy-done
  131.8 1.0 copy.14
Async XLA Ops:
  129.4 2.4 %copy-start = (bf16[3,480,384]{2,1,0:T(8,128)(2,1)S(1)}, bf16[3,480,384]{2,1,0:T(8,128)(2,1)}, u32[]{:S(2)}) copy-start(bf16[3,480,384]{2,1,0:T(8,128)(2,1)} %get-tuple-element.8) | copy-start | bytes 3317764

commit v3 on v2

--- a/solution.py
+++ b/solution.py
@@ -11,6 +11,8 @@
 NORM_EPS = 1e-05
 SCALE = HD ** (-0.5)
 PER_Z = 4
+PART = 128
+LEAST = 2
 MESH = pl.DeviceIdType.MESH
 F32 = jnp.float32
 BF16 = jnp.bfloat16
@@ -45,11 +47,11 @@
 
 
 def kernel(
-    n_sec, n_ten, width_all,
+    n_sec, n_ten, width_all, slots,
     read_in, write_in, fwd_in, stash_in, og_in, gain_in,
     act_ref, grad_ref, new_out,
-    new_ref, zeros, read_ref, write_ref, gain_ref, fwd_ref, stash_ref, og_ref, got_s, got_f, act_out, grad_out, att_f, att_b, probs_ref, low_ref, part, wide, tiles_f, tiles_b,
-    s_send, s_recv, f_send, f_recv, g_send, g_recv, a_send, a_recv, pf_send, pf_recv, pb_send, pb_recv, loads, go_sem,
+    new_ref, zeros, read_ref, write_ref, gain_ref, fwd_ref, stash_ref, og_ref, pay_ref, got_s, back_ref, gathered, packed, crossed, fan, quarters, act_out, grad_out, att_f, att_b, probs_ref, low_ref, part, wide, tiles_f, tiles_b,
+    s_send, s_recv, q_send, q_recv, c_send, c_recv, d_send, d_recv, g_send, g_recv, a_send, a_recv, pf_send, pf_recv, pb_send, pb_recv, loads, go_sem,
 ):
     length = og_ref.shape[0]
     heads = og_ref.shape[1] // HD
@@ -63,6 +65,14 @@
     layer = me_s // PER_Z
     next_to_middle = lax.rem(layer + 1, 4) < 2
     z_mate = (me_s + PER_Z * (1 - 2 * lax.rem(layer, 2)), me_t)
+    seat = lax.rem(me_s, PER_Z)
+    base = me_s - seat
+    far_base = n_sec - PER_Z - base
+    across = (far_base + seat, me_t)
+    lower = me_s < n_sec // 2
+
+    def first_row(quarter):
+        return pl.multiple_of(112 * quarter + 16 * (quarter // 2), 16)
 
     load_stash = pltpu.make_async_copy(stash_in, stash_ref, loads.at[0])
     load_fwd = pltpu.make_async_copy(fwd_in, fwd_ref, loads.at[1])
@@ -84,6 +94,9 @@
 
     greet(partner)
     greet(z_mate)
+    greet(across)
+    for step in range(1, PER_Z):
+        greet((base + lax.rem(seat + step, PER_Z), me_t))
     greet((lax.rem(me_s + 1, n_sec), me_t))
     greet((lax.rem(me_s + n_sec - 1, n_sec), me_t))
 
@@ -92,8 +105,33 @@
         return carry
 
     lax.fori_loop(1, n_ten, greet_peer, 0)
+
+    def swaps(section, is_lower):
+        return (write_ref[section] < 1) != is_lower
+
+    def partner_reads(section, is_lower):
+        return (read_ref[n_sec - 1 - section] < 1) == is_lower
+
+    def overflow(first, is_lower):
+        both = [
+            jnp.where(
+                jnp.logical_and(swaps(first + i, is_lower), partner_reads(first + i, is_lower)), 1, 0
+            )
+            for i in range(PER_Z)
+        ]
+        ranks = [sum(both[:i]) if i else jnp.int32(0) for i in range(PER_Z)]
+        return both, ranks
+
+    for load in small:
+        load.wait()
     load_stash.wait()
-    pl.semaphore_wait(barrier, n_ten + 3)
+    load_fwd.wait()
+    sends_stash = partner_reads(me_s, lower)
+    for i in range(3):
+        pay_ref[i] = jnp.where(sends_stash, stash_ref[i], fwd_ref[i])
+    both_out, rank_out = overflow(base, lower)
+    both_in, rank_in = overflow(far_base, jnp.logical_not(lower))
+    pl.semaphore_wait(barrier, n_ten + 7)
 
     def copy_to(src, dst, send, recv, device):
         return pltpu.make_async_remote_copy(
@@ -102,12 +140,36 @@
 
     def stash_copy(h):
         return copy_to(
-            stash_ref.at[:, :, cols(h)], got_s.at[:, :, cols(h)], s_send.at[h], s_recv.at[h], partner
-        )
-
-    def fwd_copy(h):
-        return copy_to(
-            fwd_ref.at[:, :, cols(h)], got_f.at[:, :, cols(h)], f_send.at[h], f_recv.at[h], partner
+            pay_ref.at[:, :, cols(h)], got_s.at[:, :, cols(h)], s_send.at[h], s_recv.at[h], partner
+        )
+
+    def quarter_copy(step):
+        other = lax.rem(seat + step, PER_Z)
+        return copy_to(
+            fwd_ref.at[:, pl.ds(first_row(other), PART), :], gathered.at[seat],
+            q_send.at[step], q_recv.at[seat], (base + other, me_t),
+        )
+
+    def quarter_arrival(step):
+        other = lax.rem(seat + step, PER_Z)
+        return copy_to(
+            fwd_ref.at[:, pl.ds(first_row(other), PART), :], gathered.at[other],
+            q_send.at[step], q_recv.at[other], (base + other, me_t),
+        )
+
+    def cross_copy(i):
+        return copy_to(packed.at[i], crossed.at[i], c_send.at[i], c_recv.at[i], across)
+
+    def fan_copy(i, step):
+        other = lax.rem(seat + step, PER_Z)
+        return copy_to(
+            fan.at[i, other], quarters.at[i, seat], d_send.at[i, step], d_recv.at[i, seat], (base + other, me_t)
+        )
+
+    def fan_arrival(i, step):
+        other = lax.rem(seat + step, PER_Z)
+        return copy_to(
+            fan.at[i, other], quarters.at[i, other], d_send.at[i, step], d_recv.at[i, other], (base + other, me_t)
         )
 
     def grad_copy(h):
@@ -151,13 +213,13 @@
     for h in range(heads):
         stash_copy(h).start()
 
+    for step in range(1, PER_Z):
+        quarter_copy(step).start()
+
     wide[...] = jnp.zeros_like(wide)
     tiles_f[me_t] = jnp.zeros((8, HD), F32)
 
-    load_fwd.wait()
     load_og.wait()
-    for load in small:
-        load.wait()
     squares = jnp.zeros((length, HD), F32)
     for h in range(heads):
         unused_a, unused_b, out = attend(fwd_ref[0, :, cols(h)], fwd_ref[1, :, cols(h)], fwd_ref[2, :, cols(h)])
@@ -186,7 +248,17 @@
         blank.start()
         blank.wait()
 
-    lower = me_s < n_sec // 2
+    gathered[seat] = fwd_ref[:, pl.ds(first_row(seat), PART), :]
+    for step in range(1, PER_Z):
+        quarter_copy(step).wait_send()
+        quarter_arrival(step).wait_recv()
+    for slot in range(slots):
+        member = sum(
+            jnp.where(jnp.logical_and(both_out[i] == 1, rank_out[i] == slot), i, 0) for i in range(1, PER_Z)
+        )
+        for i in range(3):
+            packed[i, slot] = gathered[member, i]
+
     own_read = (read_ref[me_s] < 1) == lower
     own_write = (write_ref[me_s] < 1) == lower
     squares = jnp.zeros((length, HD), F32)
@@ -199,13 +271,15 @@
             @pl.when(next_to_middle)
             def _():
                 pl.semaphore_signal(go_sem, inc=1, device_id=z_mate, device_id_type=MESH)
+                for i in range(3):
+                    cross_copy(i).start()
 
         stash_copy(h).wait_recv()
         for part_at in range(3):
-            got_s[part_at, :, cols(h)] = jnp.where(
+            back_ref[part_at, :, cols(h)] = jnp.where(
                 own_read, stash_ref[part_at, :, cols(h)], got_s[part_at, :, cols(h)]
             )
-        probs, low, out = attend(got_s[0, :, cols(h)], got_s[1, :, cols(h)], got_s[2, :, cols(h)])
+        probs, low, out = attend(back_ref[0, :, cols(h)], back_ref[1, :, cols(h)], back_ref[2, :, cols(h)])
         probs_ref[h] = probs
         low_ref[h] = low
         att_b[:, cols(h)] = out
@@ -223,26 +297,45 @@
         out = att_b[:, cols(h)]
         scaled = og_ref[:, cols(h)].astype(F32) * gain_ref[cols(h)][None, :]
         g_low = (inv_back * scaled - out * pull).astype(BF16)
-        grad_probs = nt(g_low, got_s[2, :, cols(h)])
+        grad_probs = nt(g_low, back_ref[2, :, cols(h)])
         delta = jnp.sum(g_low.astype(F32) * out, axis=-1, keepdims=True)
         grad_scores = (probs_ref[h] * (grad_probs - delta) * SCALE).astype(BF16)
-        grad_out[0, :, cols(h)] = nn(grad_scores, got_s[1, :, cols(h)]).astype(BF16)
-        grad_out[1, :, cols(h)] = tn(grad_scores, got_s[0, :, cols(h)]).astype(BF16)
+        grad_out[0, :, cols(h)] = nn(grad_scores, back_ref[1, :, cols(h)]).astype(BF16)
+        grad_out[1, :, cols(h)] = tn(grad_scores, back_ref[0, :, cols(h)]).astype(BF16)
         grad_out[2, :, cols(h)] = tn(low_ref[h], g_low).astype(BF16)
         pl.when(has_down)(lambda: grad_copy(h).start())
 
     @pl.when(jnp.logical_not(next_to_middle))
     def _():
         pl.semaphore_wait(go_sem, 1)
-
-    for h in range(heads):
-        fwd_copy(h).start()
-    for h in range(heads):
-        fwd_copy(h).wait()
-        for part_at in range(3):
-            new_ref[part_at, :, cols(h)] = jnp.where(
-                own_write, fwd_ref[part_at, :, cols(h)], got_f[part_at, :, cols(h)]
+        for i in range(3):
+            cross_copy(i).start()
+
+    for i in range(3):
+        cross_copy(i).wait()
+        for member in range(PER_Z):
+            slot = jnp.minimum(rank_in[PER_Z - 1 - member], slots - 1)
+            quarter = crossed[i, 0]
+            for other in range(1, slots):
+                quarter = jnp.where(slot == other, crossed[i, other], quarter)
+            fan[i, member] = quarter
+        for step in range(1, PER_Z):
+            fan_copy(i, step).start()
+
+    for i in range(3):
+        quarters[i, seat] = fan[i, seat]
+        for step in range(1, PER_Z):
+            fan_arrival(i, step).wait_recv()
+        for quarter in range(PER_Z):
+            rows = pl.ds(112 * quarter + 16 * (quarter // 2), PART)
+            new_ref[i, rows, :] = jnp.where(
+                own_write,
+                fwd_ref[i, rows, :],
+                jnp.where(own_read, got_s[i, rows, :], quarters[i, quarter]),
             )
+    for i in range(3):
+        for step in range(1, PER_Z):
+            fan_copy(i, step).wait_send()
 
     store = pltpu.make_async_copy(new_ref, new_out, loads.at[7])
     store.start()
@@ -268,47 +361,61 @@
     three, length, width = fwd_qkv.shape[1:]
     heads = width // HD
     dma = pltpu.SemaphoreType.DMA
-    vmem = pl.BlockSpec(memory_space=pltpu.VMEM)
-    act, grads, new = pl.pallas_call(
-        functools.partial(kernel, n_sec, n_ten, float(width * n_ten)),
-        out_shape=(
-            jax.ShapeDtypeStruct((length, width), BF16),
-            jax.ShapeDtypeStruct((three, length, width), BF16),
-            jax.ShapeDtypeStruct((three, length, width), BF16),
-        ),
-        in_specs=[pl.BlockSpec(memory_space=pl.ANY)] * 6,
-        out_specs=(pl.BlockSpec(memory_space=pl.ANY),) * 3,
-        scratch_shapes=[
-            pltpu.VMEM((three, length, width), BF16),
-            pltpu.VMEM((three, length, width), BF16),
-            pltpu.SMEM(read_slot.shape, jnp.int32),
-            pltpu.SMEM(write_slot.shape, jnp.int32),
-            pltpu.VMEM(norm_gain.shape, F32),
-            pltpu.VMEM((three, length, width), BF16),
-            pltpu.VMEM((three, length, width), BF16),
-            pltpu.VMEM((length, width), BF16),
-            pltpu.VMEM((three, length, width), BF16),
-            pltpu.VMEM((three, length, width), BF16),
-            pltpu.VMEM((length, width), BF16),
-            pltpu.VMEM((three, length, width), BF16),
-            pltpu.VMEM((length, width), F32),
-            pltpu.VMEM((length, width), F32),
-            pltpu.VMEM((heads, length, length), F32),
-            pltpu.VMEM((heads, length, length), BF16),
-            pltpu.VMEM((8, HD), F32),
-            pltpu.VMEM((4 * HD, HD), F32),
-            pltpu.VMEM((n_ten, 8, HD), F32),
-            pltpu.VMEM((n_ten, 8, HD), F32),
-            dma((heads,)), dma((heads,)), dma((heads,)), dma((heads,)), dma((heads,)), dma((heads,)),
-            dma((1,)), dma((1,)),
-            dma((n_ten,)), dma((n_ten,)), dma((n_ten,)), dma((n_ten,)),
-            dma((8,)), pltpu.SemaphoreType.REGULAR,
-        ],
-        compiler_params=pltpu.CompilerParams(
-            collective_id=0, has_side_effects=True, vmem_limit_bytes=56 * 1024 * 1024
-        ),
-        name="slot",
-    )(read_slot, write_slot, fwd_qkv[0], stash[0, 0], out_grad[0], norm_gain)
+    triple = pltpu.VMEM((three, length, width), BF16)
+
+    def call(slots):
+        return pl.pallas_call(
+            functools.partial(kernel, n_sec, n_ten, float(width * n_ten), slots),
+            out_shape=(
+                jax.ShapeDtypeStruct((length, width), BF16),
+                jax.ShapeDtypeStruct((three, length, width), BF16),
+                jax.ShapeDtypeStruct((three, length, width), BF16),
+            ),
+            in_specs=[pl.BlockSpec(memory_space=pl.ANY)] * 6,
+            out_specs=(pl.BlockSpec(memory_space=pl.ANY),) * 3,
+            scratch_shapes=[
+                triple, triple,
+                pltpu.SMEM(read_slot.shape, jnp.int32),
+                pltpu.SMEM(write_slot.shape, jnp.int32),
+                pltpu.VMEM(norm_gain.shape, F32),
+                triple, triple, pltpu.VMEM((length, width), BF16),
+                triple, triple, triple,
+                pltpu.VMEM((PER_Z, three, PART, width), BF16),
+                pltpu.VMEM((three, slots, PART, width), BF16),
+                pltpu.VMEM((three, slots, PART, width), BF16),
+                pltpu.VMEM((three, PER_Z, PART, width), BF16),
+                pltpu.VMEM((three, PER_Z, PART, width), BF16),
+                pltpu.VMEM((length, width), BF16),
+                triple,
+                pltpu.VMEM((length, width), F32),
+                pltpu.VMEM((length, width), F32),
+                pltpu.VMEM((heads, length, length), F32),
+                pltpu.VMEM((heads, length, length), BF16),
+                pltpu.VMEM((8, HD), F32),
+                pltpu.VMEM((4 * HD, HD), F32),
+                pltpu.VMEM((n_ten, 8, HD), F32),
+                pltpu.VMEM((n_ten, 8, HD), F32),
+                dma((heads,)), dma((heads,)),
+                dma((PER_Z,)), dma((PER_Z,)), dma((three,)), dma((three,)), dma((three, PER_Z)), dma((three, PER_Z)),
+                dma((heads,)), dma((heads,)), dma((1,)), dma((1,)),
+                dma((n_ten,)), dma((n_ten,)), dma((n_ten,)), dma((n_ten,)),
+                dma((8,)), pltpu.SemaphoreType.REGULAR,
+            ],
+            compiler_params=pltpu.CompilerParams(
+                collective_id=slots - LEAST, has_side_effects=True, vmem_limit_bytes=56 * 1024 * 1024
+            ),
+            name="slot%d" % slots,
+        )
+
+    here = jnp.arange(n_sec, dtype=jnp.int32)
+    lower = here < n_sec // 2
+    both = ((write_slot < 1) != lower) & ((jnp.flip(read_slot) < 1) == lower)
+    most = jnp.max(jnp.sum(both.astype(jnp.int32).reshape(-1, PER_Z), axis=1))
+    act, grads, new = lax.switch(
+        jnp.maximum(most, LEAST) - LEAST,
+        [call(slots) for slots in range(LEAST, PER_Z + 1)],
+        read_slot, write_slot, fwd_qkv[0], stash[0, 0], out_grad[0], norm_gain,
+    )
     return act[None], grads[None], new[None, None]
 
 

time: 133 us -> 139 us (1.045)
  loops' own time: 0 us -> 6.04 us
  local copies, waits for them, and re-layouts: 5.19 us -> 3.54 us
  other arithmetic: 0 us -> 1.42 us
    another operation x0 -> x1, loops' own time: none -> 6.04 us  [shards(): lax.switch(jnp.maximum(most, LEAST) - LEAST, [call(slots) for slots in ra...]
    unnamed x5 -> x3, local copies, waits for them, and re-layouts: 5.19 us -> 2.72 us
where the time goes in v3:
time: 139 us
  Pallas kernels  127 us (91%)
  loops' own time  6.04 us (4%)
  local copies, waits for them, and re-layouts  3.54 us (3%)
  other arithmetic  1.42 us (1%)
    pallas_call x1, Pallas kernels, shards(): lax.switch(jnp.maximum(most, LEAST) - LEAST, [call(slots) for slots in ra...  127 us
    another operation x1, loops' own time, shards(): lax.switch(jnp.maximum(most, LEAST) - LEAST, [call(slots) for slots in ra...  6.04 us

profile of v3, /device:TPU:199, one launch (start us, length us, event | category | flops | bytes accessed | tf_op | source)
XLA Modules:
  0.0 139.3 jit_solution(8241300022136415085)
XLA Ops:
  0.6 0.7 rev.4
  1.4 0.7 and_convert_fusion
  2.0 0.1 reshape.15
  2.1 0.1 reduce_sum.9
  2.2 0.6 reduce_max.9
  3.5 133.0 %conditional.1 = ((bf16[480,384]{1,0:T(8,128)(2,1)S(1)}, bf16[3,480,384]{2,1,0:T(8,128)(2,1)S(1)}, bf16[3,480,384]{2,1,0:T(8,128)(2,1)S(1)})) conditional(s32[]{:T(128)} %clamp.3, (s32[32]{0:T(128)}, s32[32]{0:T(128)}, bf16[3,480,384]{2,1,0:T(8,128)(2,1)}, bf16[3,480,384]{2,1,0:T(8,128)(2,1)}, bf16[480,384]{1,0:T(8,128)(2,1)}, ...), branch_computations={%region_2.3_spmd, %region_3.4_spmd, %region_4.5_spmd} | conditional | bytes 8 | solution.py:414
  9.4 127.0 %slot4.1 = (bf16[480,384]{1,0:T(8,128)(2,1)S(1)}, bf16[3,480,384]{2,1,0:T(8,128)(2,1)S(1)}, bf16[3,480,384]{2,1,0:T(8,128)(2,1)S(1)}) custom-call(s32[32]{0:T(128)} %get-tuple-element.66.read_in, s32[32]{0:T(128)} %get-tuple-element.67.write_in, bf16[3,480,384]{2,1,0:T(8,128)(2,1)} %get-tuple-element.68.fwd_in, ...), custom_call_target="tpu_custom_call" | custom-call | tf_op jit(solution)/shard_map/cond/branch_2_fun/slot4/pallas_call | solution.py:414
  136.6 0.7 copy.21
  137.3 1.0 copy.22
  138.3 1.0 copy.23

commit v4 on v3

--- a/solution.py
+++ b/solution.py
@@ -11,8 +11,8 @@
 NORM_EPS = 1e-05
 SCALE = HD ** (-0.5)
 PER_Z = 4
-PART = 128
-LEAST = 2
+PLANS = ((2, 1), (4, 2), (4, 3), (1, 1))
+PART_ROWS = {1: 480, 2: 240, 4: 128}
 MESH = pl.DeviceIdType.MESH
 F32 = jnp.float32
 BF16 = jnp.bfloat16
@@ -47,11 +47,11 @@
 
 
 def kernel(
-    n_sec, n_ten, width_all, slots,
+    n_sec, n_ten, width_all, group, slots,
     read_in, write_in, fwd_in, stash_in, og_in, gain_in,
     act_ref, grad_ref, new_out,
-    new_ref, zeros, read_ref, write_ref, gain_ref, fwd_ref, stash_ref, og_ref, pay_ref, got_s, back_ref, gathered, packed, crossed, fan, quarters, act_out, grad_out, att_f, att_b, probs_ref, low_ref, part, wide, tiles_f, tiles_b,
-    s_send, s_recv, q_send, q_recv, c_send, c_recv, d_send, d_recv, g_send, g_recv, a_send, a_recv, pf_send, pf_recv, pb_send, pb_recv, loads, go_sem,
+    new_ref, zeros, read_ref, write_ref, gain_ref, fwd_ref, stash_ref, og_ref, pay_ref, got_s, back_ref, gathered, packed, staged, crossed, fan, pieces, act_out, grad_out, att_f, att_b, probs_ref, low_ref, part, wide, tiles_f, tiles_b,
+    s_send, s_recv, q_send, q_recv, x_send, x_recv, c_send, c_recv, d_send, d_recv, g_send, g_recv, a_send, a_recv, pf_send, pf_recv, pb_send, pb_recv, loads, go_sem,
 ):
     length = og_ref.shape[0]
     heads = og_ref.shape[1] // HD
@@ -65,14 +65,20 @@
     layer = me_s // PER_Z
     next_to_middle = lax.rem(layer + 1, 4) < 2
     z_mate = (me_s + PER_Z * (1 - 2 * lax.rem(layer, 2)), me_t)
-    seat = lax.rem(me_s, PER_Z)
+    seat = lax.rem(me_s, group)
     base = me_s - seat
-    far_base = n_sec - PER_Z - base
-    across = (far_base + seat, me_t)
+    far_base = n_sec - group - base
+    across = (n_sec - PER_Z * (layer + 1) + lax.rem(me_s, PER_Z), me_t)
+    beside = (me_s + 2 * (1 - 2 * lax.rem(me_s // 2, 2)), me_t)
     lower = me_s < n_sec // 2
 
-    def first_row(quarter):
-        return pl.multiple_of(112 * quarter + 16 * (quarter // 2), 16)
+    part_rows = PART_ROWS[group]
+
+    def first_row(piece):
+        return 112 * piece + 16 * (piece // 2) if group == 4 else part_rows * piece
+
+    def rows_of(piece):
+        return pl.ds(pl.multiple_of(first_row(piece), 16), part_rows)
 
     load_stash = pltpu.make_async_copy(stash_in, stash_ref, loads.at[0])
     load_fwd = pltpu.make_async_copy(fwd_in, fwd_ref, loads.at[1])
@@ -95,8 +101,10 @@
     greet(partner)
     greet(z_mate)
     greet(across)
-    for step in range(1, PER_Z):
-        greet((base + lax.rem(seat + step, PER_Z), me_t))
+    if group == 2:
+        greet(beside)
+    for step in range(1, group):
+        greet((base + lax.rem(seat + step, group), me_t))
     greet((lax.rem(me_s + 1, n_sec), me_t))
     greet((lax.rem(me_s + n_sec - 1, n_sec), me_t))
 
@@ -117,9 +125,9 @@
             jnp.where(
                 jnp.logical_and(swaps(first + i, is_lower), partner_reads(first + i, is_lower)), 1, 0
             )
-            for i in range(PER_Z)
+            for i in range(group)
         ]
-        ranks = [sum(both[:i]) if i else jnp.int32(0) for i in range(PER_Z)]
+        ranks = [sum(both[:i]) if i else jnp.int32(0) for i in range(group)]
         return both, ranks
 
     for load in small:
@@ -131,7 +139,7 @@
         pay_ref[i] = jnp.where(sends_stash, stash_ref[i], fwd_ref[i])
     both_out, rank_out = overflow(base, lower)
     both_in, rank_in = overflow(far_base, jnp.logical_not(lower))
-    pl.semaphore_wait(barrier, n_ten + 7)
+    pl.semaphore_wait(barrier, n_ten + 3 + group + (1 if group == 2 else 0))
 
     def copy_to(src, dst, send, recv, device):
         return pltpu.make_async_remote_copy(
@@ -143,33 +151,39 @@
             pay_ref.at[:, :, cols(h)], got_s.at[:, :, cols(h)], s_send.at[h], s_recv.at[h], partner
         )
 
-    def quarter_copy(step):
-        other = lax.rem(seat + step, PER_Z)
-        return copy_to(
-            fwd_ref.at[:, pl.ds(first_row(other), PART), :], gathered.at[seat],
+    def piece_copy(step):
+        other = lax.rem(seat + step, group)
+        return copy_to(
+            fwd_ref.at[:, rows_of(other), :], gathered.at[seat],
             q_send.at[step], q_recv.at[seat], (base + other, me_t),
         )
 
-    def quarter_arrival(step):
-        other = lax.rem(seat + step, PER_Z)
-        return copy_to(
-            fwd_ref.at[:, pl.ds(first_row(other), PART), :], gathered.at[other],
+    def piece_arrival(step):
+        other = lax.rem(seat + step, group)
+        return copy_to(
+            fwd_ref.at[:, rows_of(other), :], gathered.at[other],
             q_send.at[step], q_recv.at[other], (base + other, me_t),
         )
 
     def cross_copy(i):
-        return copy_to(packed.at[i], crossed.at[i], c_send.at[i], c_recv.at[i], across)
+        if group == 1:
+            return copy_to(fwd_ref.at[i], pieces.at[i, 0], c_send.at[i], c_recv.at[i], partner)
+        ready = staged if group == 2 else packed
+        return copy_to(ready.at[i], crossed.at[i], c_send.at[i], c_recv.at[i], across)
+
+    def stage_copy(i):
+        return copy_to(packed.at[i], staged.at[i], x_send.at[i], x_recv.at[i], beside)
 
     def fan_copy(i, step):
-        other = lax.rem(seat + step, PER_Z)
-        return copy_to(
-            fan.at[i, other], quarters.at[i, seat], d_send.at[i, step], d_recv.at[i, seat], (base + other, me_t)
+        other = lax.rem(seat + step, group)
+        return copy_to(
+            fan.at[i, other], pieces.at[i, seat], d_send.at[i, step], d_recv.at[i, seat], (base + other, me_t)
         )
 
     def fan_arrival(i, step):
-        other = lax.rem(seat + step, PER_Z)
-        return copy_to(
-            fan.at[i, other], quarters.at[i, other], d_send.at[i, step], d_recv.at[i, other], (base + other, me_t)
+        other = lax.rem(seat + step, group)
+        return copy_to(
+            fan.at[i, other], pieces.at[i, other], d_send.at[i, step], d_recv.at[i, other], (base + other, me_t)
         )
 
     def grad_copy(h):
@@ -213,8 +227,8 @@
     for h in range(heads):
         stash_copy(h).start()
 
-    for step in range(1, PER_Z):
-        quarter_copy(step).start()
+    for step in range(1, group):
+        piece_copy(step).start()
 
     wide[...] = jnp.zeros_like(wide)
     tiles_f[me_t] = jnp.zeros((8, HD), F32)
@@ -248,16 +262,20 @@
         blank.start()
         blank.wait()
 
-    gathered[seat] = fwd_ref[:, pl.ds(first_row(seat), PART), :]
-    for step in range(1, PER_Z):
-        quarter_copy(step).wait_send()
-        quarter_arrival(step).wait_recv()
-    for slot in range(slots):
+    if group > 1:
+        gathered[seat] = fwd_ref[:, rows_of(seat), :]
+    for step in range(1, group):
+        piece_copy(step).wait_send()
+        piece_arrival(step).wait_recv()
+    for slot in range(slots if group > 1 else 0):
         member = sum(
-            jnp.where(jnp.logical_and(both_out[i] == 1, rank_out[i] == slot), i, 0) for i in range(1, PER_Z)
+            jnp.where(jnp.logical_and(both_out[i] == 1, rank_out[i] == slot), i, 0) for i in range(1, group)
         )
         for i in range(3):
             packed[i, slot] = gathered[member, i]
+    if group == 2:
+        for i in range(3):
+            stage_copy(i).start()
 
     own_read = (read_ref[me_s] < 1) == lower
     own_write = (write_ref[me_s] < 1) == lower
@@ -267,6 +285,9 @@
         if h == heads - 1:
             for other in range(heads):
                 stash_copy(other).wait_send()
+            if group == 2:
+                for i in range(3):
+                    stage_copy(i).wait()
 
             @pl.when(next_to_middle)
             def _():
@@ -313,28 +334,29 @@
 
     for i in range(3):
         cross_copy(i).wait()
-        for member in range(PER_Z):
-            slot = jnp.minimum(rank_in[PER_Z - 1 - member], slots - 1)
-            quarter = crossed[i, 0]
+        for member in range(group if group > 1 else 0):
+            slot = jnp.minimum(rank_in[group - 1 - member], slots - 1)
+            found = crossed[i, 0]
             for other in range(1, slots):
-                quarter = jnp.where(slot == other, crossed[i, other], quarter)
-            fan[i, member] = quarter
-        for step in range(1, PER_Z):
+                found = jnp.where(slot == other, crossed[i, other], found)
+            fan[i, member] = found
+        for step in range(1, group):
             fan_copy(i, step).start()
 
     for i in range(3):
-        quarters[i, seat] = fan[i, seat]
-        for step in range(1, PER_Z):
+        if group > 1:
+            pieces[i, seat] = fan[i, seat]
+        for step in range(1, group):
             fan_arrival(i, step).wait_recv()
-        for quarter in range(PER_Z):
-            rows = pl.ds(112 * quarter + 16 * (quarter // 2), PART)
+        for piece in range(group):
+            rows = pl.ds(first_row(piece), part_rows)
             new_ref[i, rows, :] = jnp.where(
                 own_write,
                 fwd_ref[i, rows, :],
-                jnp.where(own_read, got_s[i, rows, :], quarters[i, quarter]),
+                jnp.where(own_read, got_s[i, rows, :], pieces[i, piece]),
             )
     for i in range(3):
-        for step in range(1, PER_Z):
+        for step in range(1, group):
             fan_copy(i, step).wait_send()
 
     store = pltpu.make_async_copy(new_ref, new_out, loads.at[7])
@@ -353,6 +375,17 @@
             grad_copy(h).wait_send()
 
     store.wait()
+
+
+def hand_over(a_in, b_in, c_in, a_out, b_out, c_out, sems):
+    moves = [
+        pltpu.make_async_copy(src, dst, sems.at[i])
+        for i, (src, dst) in enumerate(((a_in, a_out), (b_in, b_out), (c_in, c_out)))
+    ]
+    for move in moves:
+        move.start()
+    for move in moves:
+        move.wait()
 
 
 def shards(fwd_qkv, stash, out_grad, norm_gain, read_slot, write_slot):
@@ -363,9 +396,10 @@
     dma = pltpu.SemaphoreType.DMA
     triple = pltpu.VMEM((three, length, width), BF16)
 
-    def call(slots):
+    def call(plan, group, slots):
+        part_rows = PART_ROWS[group]
         return pl.pallas_call(
-            functools.partial(kernel, n_sec, n_ten, float(width * n_ten), slots),
+            functools.partial(kernel, n_sec, n_ten, float(width * n_ten), group, slots),
             out_shape=(
                 jax.ShapeDtypeStruct((length, width), BF16),
                 jax.ShapeDtypeStruct((three, length, width), BF16),
@@ -380,11 +414,12 @@
                 pltpu.VMEM(norm_gain.shape, F32),
                 triple, triple, pltpu.VMEM((length, width), BF16),
                 triple, triple, triple,
-                pltpu.VMEM((PER_Z, three, PART, width), BF16),
-                pltpu.VMEM((three, slots, PART, width), BF16),
-                pltpu.VMEM((three, slots, PART, width), BF16),
-                pltpu.VMEM((three, PER_Z, PART, width), BF16),
-                pltpu.VMEM((three, PER_Z, PART, width), BF16),
+                pltpu.VMEM((group, three, part_rows, width), BF16),
+                pltpu.VMEM((three, slots, part_rows, width), BF16),
+                pltpu.VMEM((three, slots, part_rows, width), BF16),
+                pltpu.VMEM((three, slots, part_rows, width), BF16),
+                pltpu.VMEM((three, group, part_rows, width), BF16),
+                pltpu.VMEM((three, group, part_rows, width), BF16),
                 pltpu.VMEM((length, width), BF16),
                 triple,
                 pltpu.VMEM((length, width), F32),
@@ -396,26 +431,38 @@
                 pltpu.VMEM((n_ten, 8, HD), F32),
                 pltpu.VMEM((n_ten, 8, HD), F32),
                 dma((heads,)), dma((heads,)),
-                dma((PER_Z,)), dma((PER_Z,)), dma((three,)), dma((three,)), dma((three, PER_Z)), dma((three, PER_Z)),
+                dma((group,)), dma((group,)), dma((three,)), dma((three,)), dma((three,)), dma((three,)), dma((three, group)), dma((three, group)),
                 dma((heads,)), dma((heads,)), dma((1,)), dma((1,)),
                 dma((n_ten,)), dma((n_ten,)), dma((n_ten,)), dma((n_ten,)),
                 dma((8,)), pltpu.SemaphoreType.REGULAR,
             ],
             compiler_params=pltpu.CompilerParams(
-                collective_id=slots - LEAST, has_side_effects=True, vmem_limit_bytes=56 * 1024 * 1024
+                collective_id=plan, has_side_effects=True, vmem_limit_bytes=56 * 1024 * 1024
             ),
-            name="slot%d" % slots,
+            name="slot%d_%d" % (group, slots),
         )
 
     here = jnp.arange(n_sec, dtype=jnp.int32)
     lower = here < n_sec // 2
-    both = ((write_slot < 1) != lower) & ((jnp.flip(read_slot) < 1) == lower)
-    most = jnp.max(jnp.sum(both.astype(jnp.int32).reshape(-1, PER_Z), axis=1))
+    both = ((write_slot < 1) != lower) & ((read_slot < 1) != lower)
+    word = jnp.uint32
+    chips = jnp.sum(jnp.where(both, word(1) << (2 * (here // 2)).astype(word), word(0)))
+    fours = (chips & word(0x33333333)) + ((chips >> word(2)) & word(0x33333333))
+    steps = (chips & word(0xAAAAAAAA), (fours + word(0x11111111)) & word(0x44444444), fours & word(0x44444444))
     act, grads, new = lax.switch(
-        jnp.maximum(most, LEAST) - LEAST,
-        [call(slots) for slots in range(LEAST, PER_Z + 1)],
+        sum((step != 0).astype(jnp.int32) for step in steps),
+        [call(plan, group, slots) for plan, (group, slots) in enumerate(PLANS)],
         read_slot, write_slot, fwd_qkv[0], stash[0, 0], out_grad[0], norm_gain,
     )
+    act, grads, new = pl.pallas_call(
+        hand_over,
+        out_shape=tuple(jax.ShapeDtypeStruct(x.shape, x.dtype) for x in (act, grads, new)),
+        in_specs=[pl.BlockSpec(memory_space=pltpu.VMEM)] * 3,
+        out_specs=(pl.BlockSpec(memory_space=pl.ANY),) * 3,
+        scratch_shapes=[dma((3,))],
+        compiler_params=pltpu.CompilerParams(vmem_limit_bytes=56 * 1024 * 1024),
+        name="hand_over",
+    )(act, grads, new)
     return act[None], grads[None], new[None, None]
 
 

time: 139 us -> 102 us (0.73)
  Pallas kernels: 127 us -> 97.1 us
  loops' own time: 6.04 us -> 0.55 us
  local copies, waits for them, and re-layouts: 3.54 us -> 0 us
  between operations: 1.3 us -> 2.81 us
    pallas_call x1 -> x2, Pallas kernels: 127 us -> 97.1 us  [the longest x1 95.6 us: shards(): lax.switch(sum(((step != 0).astype(jnp.int32) for step in steps)), [call(...]
    another operation x1, loops' own time: 6.04 us -> 0.55 us  [shards(): lax.switch(sum(((step != 0).astype(jnp.int32) for step in steps)), [call(...]
    unnamed x3 -> x0, local copies, waits for them, and re-layouts: 2.72 us -> none
where the time goes in v4:
time: 102 us
  Pallas kernels  97.1 us (95%)
  between operations  2.81 us (3%)
  other arithmetic  1.31 us (1%)
    pallas_call x1, Pallas kernels, shards(): lax.switch(sum(((step != 0).astype(jnp.int32) for step in steps)), [call(...  95.6 us

profile of v4, /device:TPU:199, one launch (start us, length us, event | category | flops | bytes accessed | tf_op | source)
XLA Modules:
  0.0 101.8 jit_solution(11909775725851543565)
XLA Ops:
  0.6 1.3 %fusion.3 = u32[]{:T(128)} fusion(s32[32]{0:T(128)} %param.14, s32[32]{0:T(128)} %param.15), kind=kLoop, calls=%fused_computation.8 | loop fusion | flops 607 | bytes 260 | tf_op jit(solution)/shard_map/reduce_sum | solution.py:449
  3.9 96.1 %conditional.1 = ((bf16[480,384]{1,0:T(8,128)(2,1)S(1)}, bf16[3,480,384]{2,1,0:T(8,128)(2,1)S(1)}, bf16[3,480,384]{2,1,0:T(8,128)(2,1)S(1)})) conditional(s32[]{:T(128)} %clamp.3, (s32[32]{0:T(128)}, s32[32]{0:T(128)}, bf16[3,480,384]{2,1,0:T(8,128)(2,1)}, bf16[3,480,384]{2,1,0:T(8,128)(2,1)}, ...), branch_computations={%region_1.2_spmd, %region_2.3_spmd, %region_3.4_spmd, %region_4.5_... | conditional | bytes 8 | solution.py:452
  3.9 95.6 %slot2_1.1 = (bf16[480,384]{1,0:T(8,128)(2,1)S(1)}, bf16[3,480,384]{2,1,0:T(8,128)(2,1)S(1)}, bf16[3,480,384]{2,1,0:T(8,128)(2,1)S(1)}) custom-call(s32[32]{0:T(128)} %get-tuple-element.48.read_in, s32[32]{0:T(128)} %get-tuple-element.49.write_in, bf16[3,480,384]{2,1,0:T(8,128)(2,1)} %get-tuple-element.50.fwd_in, ...), custom_call_target="tpu_custom_call" | custom-call | tf_op jit(solution)/shard_map/cond/branch_0_fun/slot2_1/pallas_call | solution.py:452
  100.0 1.5 %hand_over.1 = (bf16[480,384]{1,0:T(8,128)(2,1)}, bf16[3,480,384]{2,1,0:T(8,128)(2,1)}, bf16[3,480,384]{2,1,0:T(8,128)(2,1)}) custom-call(bf16[480,384]{1,0:T(8,128)(2,1)S(1)} %get-tuple-element.81.a_in, bf16[3,480,384]{2,1,0:T(8,128)(2,1)S(1)} %get-tuple-element.82.b_in, bf16[3,480,384]{2,1,0:T(8,128)(2,1)S(1)} %get-tuple-element.83.c_in), custom_call_target="tpu_custom_call" | custom-call | tf_op jit(solution)/shard_map/hand_over/pallas_call | solution.py:457
